TPU v7x, 128 devices: a whole 4x4x4 slice. The times are simulated.
128 devices in a mesh: gx: 16 (over x, y), shot: 8 (over z, core).
Axes of the slice: x: 4, y: 4, z: 4, core: 2. Of those that a mesh axis runs over, the one named last changes fastest.
Arguments:
- wave_prev: float32 [8, 128, 512, 256], P('shot', 'gx'), may hold values from -6 to 6
- wave_now: float32 [8, 128, 512, 256], P('shot', 'gx'), may hold values from -6 to 6
- adjoint_next: float32 [8, 128, 512, 256], P('shot', 'gx'), may hold values from -6 to 6
- adjoint_now: float32 [8, 128, 512, 256], P('shot', 'gx'), may hold values from -6 to 6
- velocity: float32 [128, 512, 256], P('gx'), may hold values from 1.5 to 4.5
- observed: float32 [512, 2, 4096], P('shot', None, 'gx'), may hold values from -0.8 to 0.8
- encode_signs: int32 [8, 512], replicated, may hold values from -1 to 1, as said below
- panel_shot: int32 [512], replicated, may hold values from 0 to 511, each once
- source_position: int32 [3, 512], replicated, may hold values from 0 to 511, as said below
- wavelet: float32 [512, 2], replicated, may hold values from -16 to 16
- receivers: int32 [4096], P('gx'), may hold values from 0 to 1048327, as said below
Outputs:
- wave_next: float32 [8, 128, 512, 256], P('shot', 'gx')
- adjoint_prev: float32 [8, 128, 512, 256], P('shot', 'gx')
- gradient: float32 [128, 512, 256], P('gx', 'shot')
Inputs may be any that keep to these rules, and one draw needn't show every extreme that they name: `encode_signs`: each entry is +1 or -1. `panel_shot`: each shot appears in exactly one panel row. `source_position`: row 0 holds x cells below 128, row 1 y cells below 512, row 2 depth cells below 8. `receivers`: entry r is x * 512 * 256 + y * 256 + depth with x below 8, y below 512, depth below 8, a cell of slab r // 256.
All inputs are finite; a program needn't handle non-finite values.
Results may differ from a plain program's by a relative error of at most 0.00023.
Values sent between devices are 32-bit elements; how exact they have to be, the bound alone decides.
A program may use at most 384 MiB of HBM per device.

v0:
```python
import jax
import jax.numpy as jnp
from jax import lax
from jax.sharding import PartitionSpec as P

NT = 2


COEFS = (-205.0 / 72.0, 8.0 / 5.0, -1.0 / 5.0, 8.0 / 315.0, -1.0 / 560.0)
STEP_RATIO = 0.09


def extended_2(block, sides, width):
    for axis, dim in sides:
        count = lax.axis_size(axis)
        forward = [(i, i + 1) for i in range(count - 1)]
        backward = [(target, source) for source, target in forward]
        low = lax.ppermute(
            lax.slice_in_dim(block, block.shape[dim] - width, None, axis=dim), axis, forward
        )
        high = lax.ppermute(lax.slice_in_dim(block, 0, width, axis=dim), axis, backward)
        block = jnp.concatenate([low, block, high], axis=dim)
    return block


def stencil(extended):
    x_count = extended.shape[-3] - 8
    inner_part = extended[..., 4 : 4 + x_count, :, :]
    num_rows = inner_part.shape[-2]
    num_depth = inner_part.shape[-1]
    padding_spec = [(0, 0)] * (inner_part.ndim - 2) + [(4, 4), (4, 4)]
    padded = jnp.pad(inner_part, padding_spec)
    acc_total = 3.0 * COEFS[0] * inner_part
    for offset in range(1, 5):
        stencil_pair = (
            extended[..., 4 + offset : 4 + offset + x_count, :, :]
            + extended[..., 4 - offset : 4 - offset + x_count, :, :]
        )
        stencil_pair = (
            stencil_pair
            + padded[..., 4 + offset : 4 + offset + num_rows, 4 : 4 + num_depth]
            + padded[..., 4 - offset : 4 - offset + num_rows, 4 : 4 + num_depth]
        )
        stencil_pair = (
            stencil_pair
            + padded[..., 4 : 4 + num_rows, 4 + offset : 4 + offset + num_depth]
            + padded[..., 4 : 4 + num_rows, 4 - offset : 4 - offset + num_depth]
        )
        acc_total = acc_total + COEFS[offset] * stencil_pair
    return acc_total


def place_sources(
    sign_rows, wavelet, source_position, time_index, first_x, width, num_rows, num_depth
):
    amplitude = sign_rows * wavelet[:, time_index][None, :]
    local_x = source_position[0] - first_x
    inside = (local_x >= 0) & (local_x < width)
    clipped = jnp.clip(local_x, 0, width - 1)
    super_count = sign_rows.shape[0]
    super_index = jnp.arange(super_count, dtype=jnp.int32)[:, None]
    placed = jnp.zeros((super_count, width, num_rows, num_depth), jnp.float32)
    return placed.at[
        super_index, clipped[None, :], source_position[1][None, :], source_position[2][None, :]
    ].add(jnp.where(inside[None, :], amplitude, 0.0))


def forward_step(prev_field, now_field, courant, sources):
    extended = extended_2(now_field, (("gx", 1),), 4)
    return 2.0 * now_field - prev_field + courant * (stencil(extended) + sources)


def adjoint_step(next_field, now_field, courant, sources):
    extended = extended_2(now_field, (("gx", 1),), 4)
    return 2.0 * now_field - next_field + courant * (stencil(extended) + sources)


def per_device(
    wave_prev,
    wave_now,
    adjoint_next,
    adjoint_now,
    velocity,
    observed,
    encode_signs,
    panel_shot,
    source_position,
    wavelet,
    receivers,
):
    supers_here = wave_now.shape[0]
    x_cells = wave_now.shape[1]
    num_rows = wave_now.shape[2]
    num_depth = wave_now.shape[3]
    slab_cells = x_cells * num_rows * num_depth
    group = lax.axis_index("shot")
    first_x = lax.axis_index("gx") * x_cells
    courant = (velocity * STEP_RATIO) ** 2
    sign_float = encode_signs.astype(jnp.float32)
    my_signs = lax.dynamic_slice_in_dim(sign_float, group * supers_here, supers_here, 0)
    sign_panel = sign_float[:, panel_shot]
    my_panel_signs = lax.dynamic_slice_in_dim(sign_panel, group * supers_here, supers_here, 0)
    piece = lax.all_gather(observed, "shot", axis=0, tiled=True)
    encoded = jnp.dot(
        my_panel_signs, piece.reshape(piece.shape[0], -1), precision=lax.Precision.HIGHEST
    )
    encoded = encoded.reshape(supers_here, NT, -1)

    def sample(field):
        return field.reshape(supers_here, -1)[:, receivers]

    def inject(resid):
        return (
            jnp.zeros((supers_here, slab_cells), jnp.float32)
            .at[:, receivers]
            .add(resid)
            .reshape(supers_here, x_cells, num_rows, num_depth)
        )

    resid_one = sample(wave_now) - encoded[:, 0]
    second_sources = place_sources(
        my_signs, wavelet, source_position, 1, first_x, x_cells, num_rows, num_depth
    )
    first_sources = place_sources(
        my_signs, wavelet, source_position, 0, first_x, x_cells, num_rows, num_depth
    )
    wave_mid = forward_step(wave_prev, wave_now, courant, first_sources)
    wave_last = forward_step(wave_now, wave_mid, courant, second_sources)
    resid_two = sample(wave_mid) - encoded[:, 1]
    adjoint_mid = adjoint_step(adjoint_next, adjoint_now, courant, inject(resid_two))
    adjoint_first = adjoint_step(adjoint_now, adjoint_mid, courant, inject(resid_one))
    image = adjoint_mid * (wave_mid - 2.0 * wave_now + wave_prev) + adjoint_now * (
        wave_last - 2.0 * wave_mid + wave_now
    )
    local_image = jnp.sum(image, axis=0)
    share_rows = num_rows // lax.axis_size("shot")
    summed = lax.psum(local_image, "shot")
    summed = lax.dynamic_slice_in_dim(summed, group * share_rows, share_rows, 1)
    velocity_part = lax.dynamic_slice_in_dim(velocity, group * share_rows, share_rows, 1)
    scale = -2.0 / (velocity_part * velocity_part)
    return (wave_last, adjoint_first, scale * summed)


def solution(mesh):
    placed = (
        P("shot", "gx", None, None),
        P("shot", "gx", None, None),
        P("shot", "gx", None, None),
        P("shot", "gx", None, None),
        P("gx", None, None),
        P("shot", None, "gx"),
        P(),
        P(),
        P(),
        P(),
        P("gx"),
    )
    return jax.shard_map(
        per_device,
        mesh=mesh,
        in_specs=placed,
        out_specs=(P("shot", "gx", None, None), P("shot", "gx", None, None), P("gx", "shot", None)),
        check_vma=False,
    )
```

profile of v0, /device:TPU:102, one launch (start us, length us, event | category | flops | bytes accessed | tf_op | source)
XLA Modules:
  0.0 525.2 jit_solution(9707646918739013071)
XLA Ops:
  7.2 0.0 all-gather.2.cloned.1.call-start
  7.2 4.5 fusion.147
  11.7 3.5 collective-permute-start.1
  15.2 4.5 collective-permute-start
  19.7 0.0 all-gather.2.cloned.1.call-update
  19.7 0.0 copy-start.4
  19.7 0.0 copy-start.5
  19.7 0.0 copy-start.6
  19.8 0.0 all-reduce.6.cloned.1.call-start
  19.8 4.6 fusion.146
  24.4 1.9 collective-permute-start.5
  26.3 6.0 %collective-permute-start.4 = (f32[1,4,512,256]{3,2,1,0:T(8,128)}, f32[1,4,512,256]{3,2,1,0:T(8,128)S(1)}, u32[]{:S(2)}, u32[]{:S(2)}) collective-permute-start(f32[1,4,512,256]{3,2,1,0:T(8,128)} %get-tuple-element.10), channel_id=1, source_target_pairs={{8,0},{16,8},{24,16},{32,24},{40,32},{48,40},{56,48},{64,56},{72,6... | collective-permute-start | bytes 6291464 | tf_op jit(solution)/shard_map/ppermute | solution.py:21
  32.4 0.0 copy-start
  32.4 0.1 add_bitcast_fusion.1
  32.5 32.0 %collective-permute-done.1 = f32[1,4,512,256]{3,2,1,0:T(8,128)} collective-permute-done((f32[1,4,512,256]{3,2,1,0:T(8,128)}, f32[1,4,512,256]{3,2,1,0:T(8,128)}, u32[]{:S(2)}, u32[]{:S(2)}) %collective-permute-start.1) | collective-permute-done | bytes 2097184 | tf_op jit(solution)/shard_map/ppermute | solution.py:18
  64.6 1.7 constant_dynamic-update-slice_fusion.3
  66.3 1.0 constant_dynamic-update-slice_fusion.1
  67.4 0.0 collective-permute-done
  67.4 1.7 constant_dynamic-update-slice_fusion
  69.1 10.5 %fusion.69 = f32[8,512,256]{2,1,0:T(8,128)} fusion(f32[1,8,512,256]{3,2,1,0:T(8,128)S(1)} %copy-done, f32[1,12,512,256]{3,2,1,0:T(8,128)S(1)} %get-tuple-element.17, f32[1,12,512,256]{3,2,1,0:T(8,128)S(1)} %constant_dynamic-update-slice_fusion), kind=kLoop, calls=%fused_computation.164 | loop fusion | flops 30408704 | bytes 41943040 | tf_op jit(solution)/shard_map/add | solution.py:49
  79.6 69.9 %scatter_fusion = f32[8,512,256]{2,1,0:T(8,128)} fusion(f32[8,512,256]{2,1,0:T(8,128)} %fusion.69, s32[512]{0:T(512)S(1)} %bitcast.77, f32[512]{0:T(512)S(1)} %bitcast.85), kind=kCustom, calls=%fused_computation.3 | custom fusion | flops 512 | bytes 12288 | tf_op jit(solution)/shard_map/scatter-add | solution.py:65
  149.6 7.1 %fusion.125 = f32[1,8,512,256]{3,2,1,0:T(8,128)S(1)} fusion(f32[8,512,256]{2,1,0:T(8,128)} %scatter_fusion, f32[1,8,512,256]{3,2,1,0:T(8,128)} %param.11, f32[1,8,512,256]{3,2,1,0:T(8,128)} %param.12, f32[8,512,256]{2,1,0:T(8,128)} %param.15), kind=kLoop, calls=%fused_computation.234 | loop fusion | flops 6291456 | bytes 20971520 | tf_op jit(solution)/shard_map/add | solution.py:70
  156.6 0.0 copy-start.1
  156.7 2.8 fusion.145
  159.4 0.5 copy-done.1
  159.9 2.1 collective-permute-start.3
  162.0 6.0 %collective-permute-start.2 = (f32[1,4,512,256]{3,2,1,0:T(8,128)}, f32[1,4,512,256]{3,2,1,0:T(8,128)}, u32[]{:S(2)}, u32[]{:S(2)}) collective-permute-start(f32[1,4,512,256]{3,2,1,0:T(8,128)} %get-tuple-element.8), channel_id=1, source_target_pairs={{8,0},{16,8},{24,16},{32,24},{40,32},{48,40},{56,48},{64,56},{72,6... | collective-permute-start | bytes 6291464 | tf_op jit(solution)/shard_map/ppermute | solution.py:21
  168.1 0.1 copy.88
  168.2 0.0 copy-start.8
  168.2 0.0 copy-start.7
  168.2 6.4 %copy.96 = f32[512,2,8,128]{3,1,2,0:T(2,128)} copy(f32[512,2,8,128]{3,2,1,0:T(8,128)} %bitcast.76) | data formatting | bytes 8388608
  174.6 0.0 copy-done.8
  174.6 3.5 gather_fusion.2
  178.1 1.0 gather_fusion.1
  179.1 0.2 dynamic-slice_reduce_fusion
  179.4 0.0 all-gather.2.cloned.1.call-done
  179.4 1.8 fusion.130
  181.2 6.4 %copy.94 = f32[512,2,8,128]{3,1,2,0:T(2,128)} copy(f32[512,2,8,128]{3,2,1,0:T(8,128)} %bitcast.79) | data formatting | bytes 8388608
  187.6 3.5 gather_fusion
  191.1 4.2 scatter_custom_fusion.2
  195.3 5.2 reshape.73
  200.5 0.0 collective-permute-done.5
  200.5 1.9 constant_dynamic-update-slice_fusion.7
  202.4 0.9 copy-done.2
  203.3 3.0 constant_dynamic-update-slice_fusion.5
  206.3 2.7 copy-done.3
  208.9 0.0 collective-permute-done.4
  208.9 1.5 constant_dynamic-update-slice_fusion.4
  210.4 0.0 collective-permute-done.3
  210.4 0.3 collective-permute-done.2
  210.8 45.4 %fusion.40 = f32[8,512,256]{2,1,0:T(8,128)} fusion(f32[1,8,512,256]{3,2,1,0:T(8,128)} %copy-done.1, f32[1,4,512,256]{3,2,1,0:T(8,128)} %collective-permute-done.3, f32[1,4,512,256]{3,2,1,0:T(8,128)} %collective-permute-done.2), kind=kLoop, calls=%fused_computation.135 | loop fusion | flops 38797312 | bytes 12582912 | tf_op jit(solution)/shard_map/add | solution.py:49
  256.2 69.9 %scatter_fusion.1 = f32[8,512,256]{2,1,0:T(8,128)} fusion(f32[8,512,256]{2,1,0:T(8,128)} %fusion.40, s32[512]{0:T(512)S(1)} %bitcast.78, f32[512]{0:T(512)S(1)} %bitcast.84), kind=kCustom, calls=%fused_computation.4 | custom fusion | flops 512 | bytes 12288 | tf_op jit(solution)/shard_map/scatter-add | solution.py:65
  326.1 60.3 %add_bitcast_fusion = (f32[8,512,256]{2,1,0:T(8,128)}, f32[1,8,512,256]{3,2,1,0:T(8,128)}, f32[1,8,512,256]{3,2,1,0:T(8,128)}) fusion(f32[1,8,512,256]{3,2,1,0:T(8,128)} %param.14, f32[1,8,512,256]{3,2,1,0:T(8,128)} %param.12, f32[1,8,512,256]{3,2,1,0:T(8,128)} %param.11, f32[1,8,512,256]{3,2,1,0:T(8,128)} %copy-done.1, f32[1,8,512,256]{3,2,1,0:T(8,128)} %reshape.73, ...), kind=kLoop, calls=%fused_computation.235 | loop fusion | flops 50331648 | bytes 79691776 | tf_op jit(solution)/shard_map/reduce_sum | solution.py:135
  386.4 0.0 all-reduce.6.cloned.1.call-update
  386.4 4.6 fusion.144
  391.0 1.9 collective-permute-start.7
  392.9 6.5 %collective-permute-start.6 = (f32[1,4,512,256]{3,2,1,0:T(8,128)}, f32[1,4,512,256]{3,2,1,0:T(8,128)}, u32[]{:S(2)}, u32[]{:S(2)}) collective-permute-start(f32[1,4,512,256]{3,2,1,0:T(8,128)} %get-tuple-element.6), channel_id=1, source_target_pairs={{8,0},{16,8},{24,16},{32,24},{40,32},{48,40},{56,48},{64,56},{72,6... | collective-permute-start | bytes 6291464 | tf_op jit(solution)/shard_map/ppermute | solution.py:21
  399.4 4.1 scatter_custom_fusion.3
  403.5 5.3 %reshape.75 = f32[1,8,512,256]{3,2,1,0:T(8,128)} reshape(f32[1048576]{0:T(1024)} %scatter_custom_fusion.3) | data formatting | bytes 8388608 | tf_op jit(solution)/shard_map/reshape | solution.py:117
  408.8 50.6 %all-reduce.6.cloned.1.call-done = f32[8,512,256]{2,1,0:T(8,128)} async-done(((f32[8,512,256]{2,1,0:T(8,128)}), f32[8,512,256]{2,1,0:T(8,128)}) %all-reduce.6.cloned.1.call-update) | async-done | bytes 4194320 | tf_op jit(solution)/shard_map/psum | solution.py:137
  459.4 2.1 dynamic-slice_multiply_fusion
  461.5 0.0 collective-permute-done.7
  461.5 0.0 collective-permute-done.6
  461.5 56.8 %fusion.11 = f32[1,8,512,256]{3,2,1,0:T(8,128)} fusion(f32[1,8,512,256]{3,2,1,0:T(8,128)} %reshape.75, f32[1,8,512,256]{3,2,1,0:T(8,128)} %get-tuple-element.4, f32[1,4,512,256]{3,2,1,0:T(8,128)S(1)} %collective-permute-done.7, f32[1,4,512,256]{3,2,1,0:T(8,128)} %collective-permute-done.6, f32[1,8,512,256]{3,2,1,0:T(8,128)} %param.14, f32[8,512,256]{2,1,0:T(8,128)} %param.15), kind=kLoop, calls=%fused_computation.106 | loop fusion | flops 46137344 | bytes 25165824 | tf_op jit(solution)/shard_map/add | solution.py:75
  (16 shorter events, 0.1 us)
Async XLA Ops:
  7.2 172.2 %all-gather.2.cloned.1.call-start = ((), (), s32[]{:S(2)}) async-start(), calls=%async_computation | async-start | bytes 1179648 | tf_op jit(solution)/shard_map/all_gather | solution.py:103
  11.7 52.8 %collective-permute-start.1 = (f32[1,4,512,256]{3,2,1,0:T(8,128)}, f32[1,4,512,256]{3,2,1,0:T(8,128)}, u32[]{:S(2)}, u32[]{:S(2)}) collective-permute-start(f32[1,4,512,256]{3,2,1,0:T(8,128)} %get-tuple-element.15), channel_id=1, source_target_pairs={{0,8},{8,16},{16,24},{24,32},{32,40},{40,48},{48,56},{56,64},{64,7... | collective-permute-start | bytes 6291464 | tf_op jit(solution)/shard_map/ppermute | solution.py:18
  15.2 52.1 %collective-permute-start = (f32[1,4,512,256]{3,2,1,0:T(8,128)}, f32[1,4,512,256]{3,2,1,0:T(8,128)}, u32[]{:S(2)}, u32[]{:S(2)}) collective-permute-start(f32[1,4,512,256]{3,2,1,0:T(8,128)} %get-tuple-element.14), channel_id=1, source_target_pairs={{8,0},{16,8},{24,16},{32,24},{40,32},{48,40},{56,48},{64,56},{72,6... | collective-permute-start | bytes 6291464 | tf_op jit(solution)/shard_map/ppermute | solution.py:21
  19.7 12.6 %copy-start.4 = (s32[8,512]{1,0:T(8,128)S(1)}, s32[8,512]{1,0:T(8,128)}, u32[]{:S(2)}) copy-start(s32[8,512]{1,0:T(8,128)} %param.17) | copy-start | bytes 49156
  19.7 12.6 %copy-start.5 = (s32[3,512]{1,0:T(4,128)S(1)}, s32[3,512]{1,0:T(4,128)}, u32[]{:S(2)}) copy-start(s32[3,512]{1,0:T(4,128)} %param.19) | copy-start | bytes 18436
  19.7 12.8 %copy-start.6 = (f32[512,2]{0,1:T(2,128)S(1)}, f32[512,2]{0,1:T(2,128)}, u32[]{:S(2)}) copy-start(f32[512,2]{0,1:T(2,128)} %param.20) | copy-start | bytes 12292
  19.8 439.7 %all-reduce.6.cloned.1.call-start = ((), (), s32[]{:S(2)}) async-start(), calls=%async_computation.1 | async-start | bytes 8388608 | tf_op jit(solution)/shard_map/psum | solution.py:137
  24.4 176.1 %collective-permute-start.5 = (f32[1,4,512,256]{3,2,1,0:T(8,128)}, f32[1,4,512,256]{3,2,1,0:T(8,128)}, u32[]{:S(2)}, u32[]{:S(2)}) collective-permute-start(f32[1,4,512,256]{3,2,1,0:T(8,128)} %get-tuple-element.11), channel_id=1, source_target_pairs={{0,8},{8,16},{16,24},{24,32},{32,40},{40,48},{48,56},{56,64},{64,7... | collective-permute-start | bytes 6291464 | tf_op jit(solution)/shard_map/ppermute | solution.py:18
  26.3 182.6 %collective-permute-start.4 = (f32[1,4,512,256]{3,2,1,0:T(8,128)}, f32[1,4,512,256]{3,2,1,0:T(8,128)S(1)}, u32[]{:S(2)}, u32[]{:S(2)}) collective-permute-start(f32[1,4,512,256]{3,2,1,0:T(8,128)} %get-tuple-element.10), channel_id=1, source_target_pairs={{8,0},{16,8},{24,16},{32,24},{40,32},{48,40},{56,48},{64,56},{72,6... | collective-permute-start | bytes 6291464 | tf_op jit(solution)/shard_map/ppermute | solution.py:21
  32.4 33.9 %copy-start = (f32[1,8,512,256]{3,2,1,0:T(8,128)S(1)}, f32[1,8,512,256]{3,2,1,0:T(8,128)}, u32[]{:S(2)}) copy-start(f32[1,8,512,256]{3,2,1,0:T(8,128)} %param.12) | copy-start | bytes 12582916
  156.6 3.3 copy-start.1
  159.9 50.5 %collective-permute-start.3 = (f32[1,4,512,256]{3,2,1,0:T(8,128)}, f32[1,4,512,256]{3,2,1,0:T(8,128)}, u32[]{:S(2)}, u32[]{:S(2)}) collective-permute-start(f32[1,4,512,256]{3,2,1,0:T(8,128)} %get-tuple-element.9), channel_id=1, source_target_pairs={{0,8},{8,16},{16,24},{24,32},{32,40},{40,48},{48,56},{56,64},{64,7... | collective-permute-start | bytes 6291464 | tf_op jit(solution)/shard_map/ppermute | solution.py:18
  162.0 48.7 %collective-permute-start.2 = (f32[1,4,512,256]{3,2,1,0:T(8,128)}, f32[1,4,512,256]{3,2,1,0:T(8,128)}, u32[]{:S(2)}, u32[]{:S(2)}) collective-permute-start(f32[1,4,512,256]{3,2,1,0:T(8,128)} %get-tuple-element.8), channel_id=1, source_target_pairs={{8,0},{16,8},{24,16},{32,24},{40,32},{48,40},{56,48},{64,56},{72,6... | collective-permute-start | bytes 6291464 | tf_op jit(solution)/shard_map/ppermute | solution.py:21
  168.2 6.4 %copy-start.8 = (s32[256]{0:T(256)S(1)}, s32[256]{0:T(256)}, u32[]{:S(2)}) copy-start(s32[256]{0:T(256)} %param.21) | copy-start | bytes 3076
  168.2 6.4 %copy-start.7 = (s32[512]{0:T(512)S(1)}, s32[512]{0:T(512)}, u32[]{:S(2)}) copy-start(s32[512]{0:T(512)} %param.18) | copy-start | bytes 6148
  200.5 2.8 copy-start.2
  206.3 2.7 copy-start.3
  391.0 70.5 %collective-permute-start.7 = (f32[1,4,512,256]{3,2,1,0:T(8,128)}, f32[1,4,512,256]{3,2,1,0:T(8,128)S(1)}, u32[]{:S(2)}, u32[]{:S(2)}) collective-permute-start(f32[1,4,512,256]{3,2,1,0:T(8,128)} %get-tuple-element.7), channel_id=1, source_target_pairs={{0,8},{8,16},{16,24},{24,32},{32,40},{40,48},{48,56},{56,64},{64,7... | collective-permute-start | bytes 6291464 | tf_op jit(solution)/shard_map/ppermute | solution.py:18
  392.9 68.6 %collective-permute-start.6 = (f32[1,4,512,256]{3,2,1,0:T(8,128)}, f32[1,4,512,256]{3,2,1,0:T(8,128)}, u32[]{:S(2)}, u32[]{:S(2)}) collective-permute-start(f32[1,4,512,256]{3,2,1,0:T(8,128)} %get-tuple-element.6), channel_id=1, source_target_pairs={{8,0},{16,8},{24,16},{32,24},{40,32},{48,40},{56,48},{64,56},{72,6... | collective-permute-start | bytes 6291464 | tf_op jit(solution)/shard_map/ppermute | solution.py:21
Sparse Core Ops, SparseCore 0:
  19.8 21.7 all-gather.1
  386.5 72.8 all-reduce.5
where the time goes:
time: 533 us; the launch traced here: 525 us
  other arithmetic  331 us (62%)
  waiting for transfers between devices  83 us (16%)
  local copies, waits for them, and re-layouts  63 us (12%)
  starting transfers between devices  32.5 us (6%)
  between operations  14.4 us (3%)
    scatter-add x2, other arithmetic, place_sources(): return placed.at[super_index, clipped[None, :], source_position[1][None,...  140 us
    reduce_sum x1, other arithmetic, per_device(): local_image = jnp.sum(image, axis=0)  60.3 us
    add x1, other arithmetic, adjoint_step(): 2.0 * now_field - next_field + courant * (stencil(extended) + sources)  56.8 us
    add x2, other arithmetic, stencil(): acc_total = acc_total + COEFS[offset] * stencil_pair  55.9 us
    psum x1, waiting for transfers between devices, per_device(): summed = lax.psum(local_image, 'shot')  50.6 us
    ppermute x4, waiting for transfers between devices, extended_2(): lax.ppermute(lax.slice_in_dim(block, block.shape[dim] - width, None, axis...  32 us
    unnamed x25, local copies, waits for them, and re-layouts  24.7 us
    ppermute x4, starting transfers between devices, extended_2(): lax.ppermute(lax.slice_in_dim(block, 0, width, axis=dim), axis, backward)  23 us
  transfers between devices with their start and end apart: 10, of which 3 were waited for; matrix products, arithmetic and copies ran while one was open for 29% of the time, Pallas kernels for 0%

commit v1 on v0

v1 whole, which is shorter than its diff:
```python
import functools

import jax
import jax.numpy as jnp
from jax import lax
from jax.experimental import pallas as pl
from jax.experimental.pallas import tpu as pltpu
from jax.sharding import PartitionSpec as P

MESH = pl.DeviceIdType.MESH
HIGHEST = lax.Precision.HIGHEST
COEFS = (-205.0 / 72.0, 8.0 / 5.0, -1.0 / 5.0, 8.0 / 315.0, -1.0 / 560.0)
STEP_RATIO = 0.09
PAD = 8
ROWS = 32
LANES = 128
DEEP = 8
S0, S1, NR, D1, D2 = range(5)


def shift_depth(low, high, k, lane):
    if k > 0:
        low_r = pltpu.roll(low, LANES - k, axis=1)
        high_r = pltpu.roll(high, LANES - k, axis=1)
        keep = lane < LANES - k
        return jnp.where(keep, low_r, high_r), jnp.where(keep, high_r, 0.0)
    low_r = pltpu.roll(low, -k, axis=1)
    high_r = pltpu.roll(high, -k, axis=1)
    keep = lane >= -k
    return jnp.where(keep, low_r, 0.0), jnp.where(keep, high_r, low_r)


def kernel(
    n_gx,
    n_shot,
    wp,
    wn,
    ax,
    an,
    vel_hbm,
    obs,
    signs,
    panel,
    srcpos,
    wav,
    recv,
    out_w,
    out_a,
    out_g,
    WN,
    AN,
    WM,
    AM,
    VEL,
    IMG,
    halo,
    stage,
    recv1,
    recv2,
    compact,
    psend,
    precv,
    ograd,
    ssem,
    rsem,
    lsem,
    osem,
    esem,
    ersem,
    s1sem,
    r1sem,
    s2sem,
    r2sem,
):
    cx, ny, nz = VEL.shape
    chunks = ny // ROWS
    share = ny // n_shot
    per_block = share // ROWS
    n_z = n_shot // 2
    g = lax.axis_index("gx")
    s = lax.axis_index("shot")
    z = lax.div(s, 2)
    core = lax.rem(s, 2)
    sibling = s + 1 - 2 * core
    has = (g > 0, g < n_gx - 1)

    barrier = pltpu.get_barrier_semaphore()
    for d in range(2):

        @pl.when(has[d])
        def _():
            pl.semaphore_signal(
                barrier, inc=1, device_id=(g + 2 * d - 1, s), device_id_type=MESH
            )

    for k in range(1, n_shot):
        pl.semaphore_signal(
            barrier, inc=1, device_id=(g, lax.rem(s + k, n_shot)), device_id_type=MESH
        )
    neighbours = has[0].astype(jnp.int32) + has[1].astype(jnp.int32)
    pl.semaphore_wait(barrier, n_shot - 1 + neighbours)

    def rows_of(c, offset=0):
        return pl.ds(pl.multiple_of(c * ROWS + offset, 8), ROWS)

    def halo_copy(h, src, offset, c, d, slot):
        return pltpu.make_async_remote_copy(
            src_ref=src.at[pl.ds(4 * d, 4), rows_of(c, offset), :],
            dst_ref=halo.at[h, slot, :, rows_of(c), :],
            send_sem=ssem.at[h, d, c],
            recv_sem=rsem.at[h, slot, c],
            device_id=(g + 2 * d - 1, s),
            device_id_type=MESH,
        )

    def halo_start(h, src, offset, c):
        for d in range(2):

            @pl.when(has[d])
            def _():
                halo_copy(h, src, offset, c, d, 1 - d).start()

    def halo_wait_recv(h, src, offset, c):
        for d in range(2):

            @pl.when(has[d])
            def _():
                halo_copy(h, src, offset, c, d, d).wait_recv()

    def halo_wait_send(h, src, offset, c):
        for d in range(2):

            @pl.when(has[d])
            def _():
                halo_copy(h, src, offset, c, d, 1 - d).wait_send()

    def loop(n, body):
        def step(i, carry):
            body(i)
            return carry

        lax.fori_loop(0, n, step, 0)

    loop(chunks, lambda c: halo_start(0, wn, 0, c))

    inner = pl.ds(PAD, ny)
    loads = [
        pltpu.make_async_copy(wn, WN.at[:, inner, :], lsem.at[0]),
        pltpu.make_async_copy(vel_hbm, VEL, lsem.at[1]),
        pltpu.make_async_copy(wp, WM.at[:, inner, :], lsem.at[2]),
        pltpu.make_async_copy(an, AN.at[:, inner, :], lsem.at[3]),
        pltpu.make_async_copy(ax, AM.at[:, inner, :], lsem.at[4]),
    ]
    for copy in loads:
        copy.start()
    loop(chunks, lambda c: halo_start(1, an, 0, c))

    n_shots = signs.shape[1]
    sign_float = signs[...].astype(jnp.float32)
    shot_row = lax.broadcasted_iota(jnp.int32, (n_shots, n_shots), 0)
    pick = jnp.where(shot_row == panel[...], 1.0, 0.0)
    sign_panel = jnp.dot(sign_float, pick, preferred_element_type=jnp.float32)
    panels = obs.shape[0]
    sign_panel = pltpu.roll(sign_panel, lax.rem((n_shot - s) * panels, n_shots), axis=1)
    mine = sign_panel[:, :panels]
    n_rec = obs.shape[2]
    for t in range(2):
        part = jnp.dot(
            mine, obs[:, t, :], precision=HIGHEST, preferred_element_type=jnp.float32
        )
        for q in range(n_shot):
            psend[q, :, t * n_rec : (t + 1) * n_rec] = jnp.broadcast_to(
                part[q : q + 1, :], (8, n_rec)
            )

    def panel_copy(k):
        to = lax.rem(s + k, n_shot)
        return pltpu.make_async_remote_copy(
            src_ref=psend.at[to],
            dst_ref=precv.at[k],
            send_sem=esem.at[k],
            recv_sem=ersem.at[k],
            device_id=(g, to),
            device_id_type=MESH,
        )

    for k in range(1, n_shot):
        panel_copy(k).start()

    for field in (WN, AN, WM, AM):
        field[:, 0:PAD, :] = jnp.zeros((cx, PAD, nz), jnp.float32)
        field[:, PAD + ny : 2 * PAD + ny, :] = jnp.zeros((cx, PAD, nz), jnp.float32)
    for d in range(2):

        @pl.when(jnp.logical_not(has[d]))
        def _():
            def clear(i):
                for h in range(4):
                    halo[h, d, :, pl.ds(pl.multiple_of(i * 8, 8), 8), :] = jnp.zeros(
                        (4, 8, nz), jnp.float32
                    )

            loop(ny // 8, clear)

    def one_hot_rows(y):
        return jnp.where(
            lax.broadcasted_iota(jnp.int32, (ny, y.shape[1]), 0) == y, 1.0, 0.0
        )

    def spread(y_hot, values, code):
        slots = lax.broadcasted_iota(jnp.int32, (LANES, code.shape[1]), 0) == code
        return lax.dot_general(
            y_hot,
            jnp.where(slots, values, 0.0),
            (((1,), (1,)), ((), ())),
            precision=HIGHEST,
            preferred_element_type=jnp.float32,
        )

    my_sign = signs[pl.ds(s, 1), :].astype(jnp.float32)
    eye = jnp.where(
        lax.broadcasted_iota(jnp.int32, (8, 2), 0)
        == lax.broadcasted_iota(jnp.int32, (8, 2), 1),
        1.0,
        0.0,
    )
    wave_rows = lax.dot_general(
        eye,
        wav[...],
        (((1,), (1,)), ((), ())),
        precision=HIGHEST,
        preferred_element_type=jnp.float32,
    )
    src_x = srcpos[0:1, :] - g * cx
    inside = (src_x >= 0) & (src_x < cx)
    src_code = jnp.where(inside, src_x * DEEP + srcpos[2:3, :], -1)
    src_hot = one_hot_rows(srcpos[1:2, :])
    compact[S0] = spread(src_hot, my_sign * wave_rows[0:1, :], src_code)
    compact[S1] = spread(src_hot, my_sign * wave_rows[1:2, :], src_code)

    flat = recv[...]
    rec_depth = lax.rem(flat, nz)
    rec_y = lax.rem(lax.div(flat, nz), ny)
    rec_x = lax.div(flat, nz * ny)
    rec_code = rec_x * DEEP + rec_depth
    rec_hot = one_hot_rows(rec_y)
    compact[NR] = spread(rec_hot, jnp.ones((1, n_rec), jnp.float32), rec_code)

    total = psend[s]
    for k in range(1, n_shot):
        panel_copy(k).wait_recv()
        total = total + precv[k]
    compact[D1] = spread(rec_hot, total[0:1, :n_rec], rec_code)
    compact[D2] = spread(rec_hot, total[0:1, n_rec:], rec_code)

    lane = lax.broadcasted_iota(jnp.int32, (8, LANES), 1)
    deep = lane < DEEP

    def laplacian(field, h, x, row):
        def plane(p, half):
            cols = pl.ds(half * LANES, LANES)
            at = pl.ds(pl.multiple_of(row, 8), 8)
            if p < 0:
                return halo[h, 0, p + 4, at, cols]
            if p >= cx:
                return halo[h, 1, p - cx, at, cols]
            return field[p, pl.ds(pl.multiple_of(row + PAD, 8), 8), cols]

        near = pl.ds(pl.multiple_of(row, 8), 8 + 2 * PAD)
        tall = [field[x, near, pl.ds(half * LANES, LANES)] for half in range(2)]

        def moved(k, half):
            return tall[half][PAD + k : PAD + k + 8]

        centre = [plane(x, 0), plane(x, 1)]
        total = [3.0 * COEFS[0] * v for v in centre]
        for k in range(1, 5):
            up = shift_depth(centre[0], centre[1], k, lane)
            down = shift_depth(centre[0], centre[1], -k, lane)
            for half in range(2):
                pair = plane(x + k, half) + plane(x - k, half)
                pair = pair + (moved(k, half) + moved(-k, half))
                pair = pair + (up[half] + down[half])
                total[half] = total[half] + COEFS[k] * pair
        return centre, total

    def compact_at(which, x, row):
        v = compact[which, pl.ds(pl.multiple_of(row, 8), 8), :]
        if x:
            v = pltpu.roll(v, LANES - DEEP * x, axis=1)
        return v

    def courant_at(x, row, half):
        v = VEL[x, pl.ds(pl.multiple_of(row, 8), 8), pl.ds(half * LANES, LANES)]
        v = v * STEP_RATIO
        return v * v

    halves = (pl.ds(0, LANES), pl.ds(LANES, LANES))

    def over_rows(c, body):
        def block(i):
            row = c * ROWS + i * 8
            for x in range(cx):
                body(x, row, i)

        loop(ROWS // 8, block)

    def here(row):
        return pl.ds(pl.multiple_of(row, 8), 8)

    def padded(row):
        return pl.ds(pl.multiple_of(row + PAD, 8), 8)

    for i in (0, 1, 2):
        loads[i].wait()

    def first(x, row, i):
        centre, lap = laplacian(WN, 0, x, row)
        lap[0] = lap[0] + jnp.where(deep, compact_at(S0, x, row), 0.0)
        for half in range(2):
            change = courant_at(x, row, half) * lap[half]
            at = (x, padded(row), halves[half])
            WM[at] = 2.0 * centre[half] - WM[at] + change
            IMG[x, here(row), halves[half]] = change

    def first_chunk(c):
        halo_wait_recv(0, wn, 0, c)
        over_rows(c, first)
        halo_start(2, WM, PAD, c)

    loop(chunks, first_chunk)

    for i in (3, 4):
        loads[i].wait()

    def second(x, row, i):
        centre, lap = laplacian(AN, 1, x, row)
        inject = compact_at(NR, x, row) * WM[x, padded(row), halves[0]] - compact_at(D2, x, row)
        lap[0] = lap[0] + jnp.where(deep, inject, 0.0)
        for half in range(2):
            at = (x, padded(row), halves[half])
            value = 2.0 * centre[half] - AM[at] + courant_at(x, row, half) * lap[half]
            AM[at] = value
            at = (x, here(row), halves[half])
            IMG[at] = IMG[at] * value

    def second_chunk(c):
        halo_wait_recv(1, an, 0, c)
        over_rows(c, second)
        halo_start(3, AM, PAD, c)

    loop(chunks, second_chunk)

    def out_copy(o, out, c):
        slot = lax.rem(c, 2)
        return pltpu.make_async_copy(
            stage.at[o, slot], out.at[:, rows_of(c), :], osem.at[o, slot]
        )

    def pair_copy(j, block):
        return pltpu.make_async_remote_copy(
            src_ref=IMG.at[:, pl.ds(pl.multiple_of(block * share, 8), share), :],
            dst_ref=recv1.at[j],
            send_sem=s1sem.at[j],
            recv_sem=r1sem.at[j],
            device_id=(g, sibling),
            device_id_type=MESH,
        )

    def ring_copy(j, slot):
        return pltpu.make_async_remote_copy(
            src_ref=IMG.at[
                :, pl.ds(pl.multiple_of((2 * j + core) * share, 8), share), :
            ],
            dst_ref=recv2.at[slot],
            send_sem=s2sem.at[j],
            recv_sem=r2sem.at[slot],
            device_id=(g, 2 * j + core),
            device_id_type=MESH,
        )

    def image_share(j):
        pair_copy(j, 2 * j + 1 - core).wait_recv()
        block = 2 * j + core

        def add(i):
            for x in range(cx):
                at = (x, pl.ds(pl.multiple_of(block * share + i * 8, 8), 8), slice(None))
                IMG[at] = IMG[at] + recv1[j, x, pl.ds(pl.multiple_of(i * 8, 8), 8), :]

        loop(share // 8, add)

        @pl.when(j != z)
        def _():
            ring_copy(j, z).start()

    def third(slot):
        def body(x, row, i):
            centre, lap = laplacian(WM, 2, x, row)
            lap[0] = lap[0] + jnp.where(deep, compact_at(S1, x, row), 0.0)
            for half in range(2):
                change = courant_at(x, row, half) * lap[half]
                at = (x, padded(row), halves[half])
                stage[0, slot, x, pl.ds(pl.multiple_of(i * 8, 8), 8), halves[half]] = (
                    2.0 * centre[half] - WN[at] + change
                )
                image = (x, here(row), halves[half])
                IMG[image] = IMG[image] + AN[at] * change

        return body

    def third_chunk(c):
        halo_wait_recv(2, WM, PAD, c)

        @pl.when(c >= 2)
        def _():
            out_copy(0, out_w, c - 2).wait()

        over_rows(c, third(lax.rem(c, 2)))
        out_copy(0, out_w, c).start()

    def third_block(b):
        for i in range(per_block):
            third_chunk(b * per_block + i)

        @pl.when(lax.rem(b, 2) != core)
        def _():
            pair_copy(lax.div(b, 2), b).start()

        @pl.when((lax.rem(b, 2) == 0) & (b >= 2))
        def _():
            image_share(lax.div(b, 2) - 1)

    loop(n_shot, third_block)
    image_share(n_z - 1)

    def fourth(slot):
        def body(x, row, i):
            centre, lap = laplacian(AM, 3, x, row)
            inject = compact_at(NR, x, row) * WN[x, padded(row), halves[0]] - compact_at(D1, x, row)
            lap[0] = lap[0] + jnp.where(deep, inject, 0.0)
            for half in range(2):
                at = (x, padded(row), halves[half])
                stage[1, slot, x, pl.ds(pl.multiple_of(i * 8, 8), 8), halves[half]] = (
                    2.0 * centre[half] - AN[at] + courant_at(x, row, half) * lap[half]
                )

        return body

    def fourth_chunk(c):
        halo_wait_recv(3, AM, PAD, c)

        @pl.when(c >= 2)
        def _():
            out_copy(1, out_a, c - 2).wait()

        over_rows(c, fourth(lax.rem(c, 2)))
        out_copy(1, out_a, c).start()

    def finish_image():
        for k in range(1, n_z):
            ring_copy(lax.rem(z + k, n_z), lax.rem(z + k, n_z)).wait_recv()

        def add(i):
            at8 = pl.ds(pl.multiple_of(i * 8, 8), 8)
            for x in range(cx):
                at = (x, pl.ds(pl.multiple_of(s * share + i * 8, 8), 8), slice(None))
                value = IMG[at]
                for k in range(1, n_z):
                    value = value + recv2[lax.rem(z + k, n_z), x, at8, :]
                v = VEL[at]
                ograd[x, at8, :] = (-2.0 / (v * v)) * value

        loop(share // 8, add)
        pltpu.make_async_copy(ograd, out_g, lsem.at[5]).start()

    def fourth_step(c):
        @pl.when(c == chunks - 2)
        def _():
            finish_image()

        fourth_chunk(c)

    loop(chunks, fourth_step)

    for o, out in ((0, out_w), (1, out_a)):
        for c in (chunks - 2, chunks - 1):
            out_copy(o, out, c).wait()
    pltpu.make_async_copy(ograd, out_g, lsem.at[5]).wait()
    for k in range(1, n_shot):
        panel_copy(k).wait_send()
    for j in range(n_z):
        pair_copy(j, 2 * j + 1 - core).wait_send()

        @pl.when(j != z)
        def _():
            ring_copy(j, z).wait_send()

    def drain(c):
        halo_wait_send(0, wn, 0, c)
        halo_wait_send(1, an, 0, c)
        halo_wait_send(2, WM, PAD, c)
        halo_wait_send(3, AM, PAD, c)

    loop(chunks, drain)


def per_device(n_gx, n_shot, wp, wn, ax, an, velocity, obs, signs, panel, srcpos, wav, recv):
    cx, ny, nz = velocity.shape
    chunks = ny // ROWS
    share = ny // n_shot
    n_z = n_shot // 2
    f32 = jnp.float32
    any_space = pl.BlockSpec(memory_space=pl.ANY)
    vmem = pl.BlockSpec(memory_space=pltpu.VMEM)
    field = (cx, ny + 2 * PAD, nz)
    dma = pltpu.SemaphoreType.DMA
    n_rec = recv.shape[0]
    cells = cx * ny * nz
    out_w, out_a, out_g = pl.pallas_call(
        functools.partial(kernel, n_gx, n_shot),
        out_shape=(
            jax.ShapeDtypeStruct((cx, ny, nz), f32),
            jax.ShapeDtypeStruct((cx, ny, nz), f32),
            jax.ShapeDtypeStruct((cx, share, nz), f32),
        ),
        in_specs=[any_space] * 5 + [vmem] * 6,
        out_specs=(any_space,) * 3,
        scratch_shapes=[
            pltpu.VMEM(field, f32),
            pltpu.VMEM(field, f32),
            pltpu.VMEM(field, f32),
            pltpu.VMEM(field, f32),
            pltpu.VMEM((cx, ny, nz), f32),
            pltpu.VMEM((cx, ny, nz), f32),
            pltpu.VMEM((4, 2, 4, ny, nz), f32),
            pltpu.VMEM((2, 2, cx, ROWS, nz), f32),
            pltpu.VMEM((n_z, cx, share, nz), f32),
            pltpu.VMEM((n_z, cx, share, nz), f32),
            pltpu.VMEM((5, ny, LANES), f32),
            pltpu.VMEM((n_shot, 8, 2 * n_rec), f32),
            pltpu.VMEM((n_shot, 8, 2 * n_rec), f32),
            pltpu.VMEM((cx, share, nz), f32),
            dma((4, 2, chunks)),
            dma((4, 2, chunks)),
            dma((6,)),
            dma((2, 2)),
            dma((n_shot,)),
            dma((n_shot,)),
            dma((n_z,)),
            dma((n_z,)),
            dma((n_z,)),
            dma((n_z,)),
        ],
        compiler_params=pltpu.CompilerParams(
            collective_id=0, has_side_effects=True, vmem_limit_bytes=60 * 2**20
        ),
        cost_estimate=pl.CostEstimate(
            flops=4 * 30 * cells, bytes_accessed=4 * 8 * cells, transcendentals=0
        ),
    )(
        wp.reshape(cx, ny, nz),
        wn.reshape(cx, ny, nz),
        ax.reshape(cx, ny, nz),
        an.reshape(cx, ny, nz),
        velocity,
        obs,
        signs,
        panel.reshape(1, -1),
        srcpos,
        wav,
        recv.reshape(1, -1),
    )
    return out_w[None], out_a[None], out_g


def solution(mesh):
    fields = P("shot", "gx", None, None)
    return jax.shard_map(
        functools.partial(per_device, mesh.shape["gx"], mesh.shape["shot"]),
        mesh=mesh,
        in_specs=(fields,) * 4
        + (P("gx", None, None), P("shot", None, "gx"), P(), P(), P(), P(), P("gx")),
        out_specs=(fields, fields, P("gx", "shot", None)),
        check_vma=False,
    )
```

time: 533 us -> 204 us (0.38)
  other arithmetic: 331 us -> 0 us
  Pallas kernels: 0 us -> 190 us
  waiting for transfers between devices: 83 us -> 0 us
  local copies, waits for them, and re-layouts: 63 us -> 9.01 us
  starting transfers between devices: 32.5 us -> 0 us
  between operations: 14.4 us -> 0.65 us
    pallas_call x0 -> x1, Pallas kernels: none -> 190 us  [per_device(): pl.pallas_call(functools.partial(kernel, n_gx, n_shot), out_shape=(jax.Sh...]
    scatter-add x4 -> x0, other arithmetic: 148 us -> none  [the longest x2 140 us: place_sources(): return placed.at[super_index, clipped[None, :], source_position[1][None,...]
    add x4 -> x0, other arithmetic: 120 us -> none  [the longest x1 56.8 us: adjoint_step(): 2.0 * now_field - next_field + courant * (stencil(extended) + sources)]
    reduce_sum x1 -> x0, other arithmetic: 60.3 us -> none  [per_device(): local_image = jnp.sum(image, axis=0)]
    psum x1 -> x0, waiting for transfers between devices: 50.6 us -> none  [per_device(): summed = lax.psum(local_image, 'shot')]
    ppermute x8 -> x0, starting transfers between devices: 32.4 us -> none  [the longest x4 23 us: extended_2(): lax.ppermute(lax.slice_in_dim(block, 0, width, axis=dim), axis, backward)]
    ppermute x8 -> x0, waiting for transfers between devices: 32.4 us -> none  [the longest x4 32 us: extended_2(): lax.ppermute(lax.slice_in_dim(block, block.shape[dim] - width, None, axis...]
    slice x4 -> x0, local copies, waits for them, and re-layouts: 16.4 us -> none  [extended_2(): lax.slice_in_dim(block, 0, width, axis=dim)]
  transfers between devices with their start and end apart: 10 -> 0, of which waited for: 3 -> 0; matrix products, arithmetic and copies ran while one was open for 29% -> 0% of each run, Pallas kernels for 0% -> 0%
where the time goes in v1:
time: 204 us; the launch traced here: 200 us
  Pallas kernels  190 us (93%)
  local copies, waits for them, and re-layouts  9.01 us (4%)
    pallas_call x1, Pallas kernels, per_device(): pl.pallas_call(functools.partial(kernel, n_gx, n_shot), out_shape=(jax.Sh...  190 us
    unnamed x8, local copies, waits for them, and re-layouts  9.01 us

profile of v1, /device:TPU:102, one launch (start us, length us, event | category | flops | bytes accessed | tf_op | source)
XLA Modules:
  0.0 200.0 jit_solution(13563846433548036956)
XLA Ops:
  0.6 1.5 copy.14.wav
  2.2 190.4 %shard_map.130 = (f32[8,512,256]{2,1,0:T(8,128)}, f32[8,512,256]{2,1,0:T(8,128)}, f32[8,64,256]{2,1,0:T(8,128)}) custom-call(f32[8,512,256]{2,1,0:T(8,128)} %bitcast.10, f32[8,512,256]{2,1,0:T(8,128)} %bitcast.11, f32[8,512,256]{2,1,0:T(8,128)} %bitcast.12, f32[8,512,256]{2,1,0:T(8,128)} %bitcast.13, f32[8,512,256]{2,1,0:T(8,128)} %vel_hbm.1, ...), custom_call_target="tpu_custom_call" | custom-call | flops 125829120 | bytes 33554432 | tf_op jit(solution)/shard_map/pallas_call | solution.py:520
  192.6 0.0 copy-start
  192.6 4.7 %copy.18 = f32[1,8,512,256]{3,2,1,0:T(8,128)} copy(f32[1,8,512,256]{3,2,1,0:T(8,128)} %bitcast.9) | data formatting | bytes 8388608
  197.2 0.0 copy-done
  197.2 0.0 copy-start.1
  197.2 2.0 %copy.19 = f32[1,8,512,256]{3,2,1,0:T(8,128)} copy(f32[1,8,512,256]{3,2,1,0:T(8,128)S(1)} %bitcast.8) | data formatting | bytes 8388608
  199.2 0.0 copy-done.1
  199.2 0.8 copy.20
Async XLA Ops:
  192.6 4.7 %copy-start = (f32[8,512,256]{2,1,0:T(8,128)S(1)}, f32[8,512,256]{2,1,0:T(8,128)}, u32[]{:S(2)}) copy-start(f32[8,512,256]{2,1,0:T(8,128)} %get-tuple-element.7) | copy-start | bytes 12582916
  197.2 2.0 %copy-start.1 = (f32[8,64,256]{2,1,0:T(8,128)S(1)}, f32[8,64,256]{2,1,0:T(8,128)}, u32[]{:S(2)}) copy-start(f32[8,64,256]{2,1,0:T(8,128)} %get-tuple-element.14) | copy-start | bytes 1572868

commit v2 on v1

--- a/solution.py
+++ b/solution.py
@@ -12,7 +12,7 @@
 COEFS = (-205.0 / 72.0, 8.0 / 5.0, -1.0 / 5.0, 8.0 / 315.0, -1.0 / 560.0)
 STEP_RATIO = 0.09
 PAD = 8
-ROWS = 32
+ROWS = 64
 LANES = 128
 DEEP = 8
 S0, S1, NR, D1, D2 = range(5)
@@ -30,48 +30,13 @@
     return jnp.where(keep, low_r, 0.0), jnp.where(keep, high_r, low_r)
 
 
-def kernel(
-    n_gx,
-    n_shot,
-    wp,
-    wn,
-    ax,
-    an,
-    vel_hbm,
-    obs,
-    signs,
-    panel,
-    srcpos,
-    wav,
-    recv,
-    out_w,
-    out_a,
-    out_g,
-    WN,
-    AN,
-    WM,
-    AM,
-    VEL,
-    IMG,
-    halo,
-    stage,
-    recv1,
-    recv2,
-    compact,
-    psend,
-    precv,
-    ograd,
-    ssem,
-    rsem,
-    lsem,
-    osem,
-    esem,
-    ersem,
-    s1sem,
-    r1sem,
-    s2sem,
-    r2sem,
-):
+def kernel(n_gx, n_shot, *refs):
+    (wp, wn, ax, an, vel_hbm), small = refs[:5], refs[5:11]
+    out_w, out_a, ograd = refs[11:14]
+    WN, AN, WM, AM, VEL, IMG, halo, recv1, recv2, compact, psend, precv = refs[14:26]
+    small_vmem = refs[26:32]
+    obs, signs, panel, srcpos, wav, recv = small_vmem
+    ssem, rsem, lsem, isem, esem, ersem, s1sem, r1sem, s2sem, r2sem, ready = refs[32:]
     cx, ny, nz = VEL.shape
     chunks = ny // ROWS
     share = ny // n_shot
@@ -84,6 +49,7 @@
     sibling = s + 1 - 2 * core
     has = (g > 0, g < n_gx - 1)
 
+    rank = 2 * z + 1 - core
     barrier = pltpu.get_barrier_semaphore()
     for d in range(2):
 
@@ -93,12 +59,23 @@
                 barrier, inc=1, device_id=(g + 2 * d - 1, s), device_id_type=MESH
             )
 
-    for k in range(1, n_shot):
-        pl.semaphore_signal(
-            barrier, inc=1, device_id=(g, lax.rem(s + k, n_shot)), device_id_type=MESH
-        )
+    def peer(r):
+        return 2 * lax.div(r, 2) + 1 - lax.rem(r, 2)
+
+    for r in range(1, n_shot):
+
+        @pl.when(rank < r)
+        def _():
+            pl.semaphore_signal(barrier, inc=1, device_id=(g, peer(r)), device_id_type=MESH)
+
+    gathers = [
+        pltpu.make_async_copy(source, target, isem.at[i])
+        for i, (source, target) in enumerate(zip(small, small_vmem))
+    ]
+    for copy in gathers:
+        copy.start()
     neighbours = has[0].astype(jnp.int32) + has[1].astype(jnp.int32)
-    pl.semaphore_wait(barrier, n_shot - 1 + neighbours)
+    pl.semaphore_wait(barrier, neighbours + rank)
 
     def rows_of(c, offset=0):
         return pl.ds(pl.multiple_of(c * ROWS + offset, 8), ROWS)
@@ -154,7 +131,15 @@
     for copy in loads:
         copy.start()
     loop(chunks, lambda c: halo_start(1, an, 0, c))
-
+    for r in range(n_shot - 1):
+
+        @pl.when(rank > r)
+        def _():
+            pl.semaphore_signal(ready, inc=1, device_id=(g, peer(r)), device_id_type=MESH)
+
+
+    for copy in gathers:
+        copy.wait()
     n_shots = signs.shape[1]
     sign_float = signs[...].astype(jnp.float32)
     shot_row = lax.broadcasted_iota(jnp.int32, (n_shots, n_shots), 0)
@@ -184,6 +169,11 @@
             device_id_type=MESH,
         )
 
+
+    @pl.when(rank < n_shot - 1)
+    def _():
+        pl.semaphore_wait(ready, n_shot - 1 - rank)
+
     for k in range(1, n_shot):
         panel_copy(k).start()
 
@@ -218,19 +208,7 @@
         )
 
     my_sign = signs[pl.ds(s, 1), :].astype(jnp.float32)
-    eye = jnp.where(
-        lax.broadcasted_iota(jnp.int32, (8, 2), 0)
-        == lax.broadcasted_iota(jnp.int32, (8, 2), 1),
-        1.0,
-        0.0,
-    )
-    wave_rows = lax.dot_general(
-        eye,
-        wav[...],
-        (((1,), (1,)), ((), ())),
-        precision=HIGHEST,
-        preferred_element_type=jnp.float32,
-    )
+    wave_rows = wav[...]
     src_x = srcpos[0:1, :] - g * cx
     inside = (src_x >= 0) & (src_x < cx)
     src_code = jnp.where(inside, src_x * DEEP + srcpos[2:3, :], -1)
@@ -260,10 +238,8 @@
         def plane(p, half):
             cols = pl.ds(half * LANES, LANES)
             at = pl.ds(pl.multiple_of(row, 8), 8)
-            if p < 0:
-                return halo[h, 0, p + 4, at, cols]
-            if p >= cx:
-                return halo[h, 1, p - cx, at, cols]
+            if p < 0 or p >= cx:
+                return 0.0 if h is None else halo[h, int(p >= cx), p % cx % 4, at, cols]
             return field[p, pl.ds(pl.multiple_of(row + PAD, 8), 8), cols]
 
         near = pl.ds(pl.multiple_of(row, 8), 8 + 2 * PAD)
@@ -351,12 +327,6 @@
 
     loop(chunks, second_chunk)
 
-    def out_copy(o, out, c):
-        slot = lax.rem(c, 2)
-        return pltpu.make_async_copy(
-            stage.at[o, slot], out.at[:, rows_of(c), :], osem.at[o, slot]
-        )
-
     def pair_copy(j, block):
         return pltpu.make_async_remote_copy(
             src_ref=IMG.at[:, pl.ds(pl.multiple_of(block * share, 8), share), :],
@@ -394,30 +364,19 @@
         def _():
             ring_copy(j, z).start()
 
-    def third(slot):
-        def body(x, row, i):
-            centre, lap = laplacian(WM, 2, x, row)
-            lap[0] = lap[0] + jnp.where(deep, compact_at(S1, x, row), 0.0)
-            for half in range(2):
-                change = courant_at(x, row, half) * lap[half]
-                at = (x, padded(row), halves[half])
-                stage[0, slot, x, pl.ds(pl.multiple_of(i * 8, 8), 8), halves[half]] = (
-                    2.0 * centre[half] - WN[at] + change
-                )
-                image = (x, here(row), halves[half])
-                IMG[image] = IMG[image] + AN[at] * change
-
-        return body
+    def third(x, row, i):
+        centre, lap = laplacian(WM, 2, x, row)
+        lap[0] = lap[0] + jnp.where(deep, compact_at(S1, x, row), 0.0)
+        for half in range(2):
+            change = courant_at(x, row, half) * lap[half]
+            at = (x, padded(row), halves[half])
+            image = (x, here(row), halves[half])
+            out_w[image] = 2.0 * centre[half] - WN[at] + change
+            IMG[image] = IMG[image] + AN[at] * change
 
     def third_chunk(c):
         halo_wait_recv(2, WM, PAD, c)
-
-        @pl.when(c >= 2)
-        def _():
-            out_copy(0, out_w, c - 2).wait()
-
-        over_rows(c, third(lax.rem(c, 2)))
-        out_copy(0, out_w, c).start()
+        over_rows(c, third)
 
     def third_block(b):
         for i in range(per_block):
@@ -434,28 +393,32 @@
     loop(n_shot, third_block)
     image_share(n_z - 1)
 
-    def fourth(slot):
-        def body(x, row, i):
-            centre, lap = laplacian(AM, 3, x, row)
-            inject = compact_at(NR, x, row) * WN[x, padded(row), halves[0]] - compact_at(D1, x, row)
-            lap[0] = lap[0] + jnp.where(deep, inject, 0.0)
-            for half in range(2):
-                at = (x, padded(row), halves[half])
-                stage[1, slot, x, pl.ds(pl.multiple_of(i * 8, 8), 8), halves[half]] = (
-                    2.0 * centre[half] - AN[at] + courant_at(x, row, half) * lap[half]
-                )
-
-        return body
+    def fourth(x, row, i):
+        centre, lap = laplacian(AM, None, x, row)
+        inject = compact_at(NR, x, row) * WN[x, padded(row), halves[0]] - compact_at(D1, x, row)
+        lap[0] = lap[0] + jnp.where(deep, inject, 0.0)
+        for half in range(2):
+            out_a[x, here(row), halves[half]] = (
+                2.0 * centre[half]
+                - AN[x, padded(row), halves[half]]
+                + courant_at(x, row, half) * lap[half]
+            )
+
+    loop(chunks, lambda c: over_rows(c, fourth))
+
+    def fourth_halo(x, row, i):
+        side = int(x >= cx // 2)
+        for half in range(2):
+            more = 0.0
+            for k in range(cx - x if side else x + 1, 5):
+                p = x + k - cx if side else x - k + 4
+                more = more + COEFS[k] * halo[3, side, p, here(row), halves[half]]
+            at = (x, here(row), halves[half])
+            out_a[at] = out_a[at] + courant_at(x, row, half) * more
 
     def fourth_chunk(c):
         halo_wait_recv(3, AM, PAD, c)
-
-        @pl.when(c >= 2)
-        def _():
-            out_copy(1, out_a, c - 2).wait()
-
-        over_rows(c, fourth(lax.rem(c, 2)))
-        out_copy(1, out_a, c).start()
+        over_rows(c, fourth_halo)
 
     def finish_image():
         for k in range(1, n_z):
@@ -472,10 +435,9 @@
                 ograd[x, at8, :] = (-2.0 / (v * v)) * value
 
         loop(share // 8, add)
-        pltpu.make_async_copy(ograd, out_g, lsem.at[5]).start()
 
     def fourth_step(c):
-        @pl.when(c == chunks - 2)
+        @pl.when(c == chunks - 1)
         def _():
             finish_image()
 
@@ -483,10 +445,6 @@
 
     loop(chunks, fourth_step)
 
-    for o, out in ((0, out_w), (1, out_a)):
-        for c in (chunks - 2, chunks - 1):
-            out_copy(o, out, c).wait()
-    pltpu.make_async_copy(ograd, out_g, lsem.at[5]).wait()
     for k in range(1, n_shot):
         panel_copy(k).wait_send()
     for j in range(n_z):
@@ -503,6 +461,19 @@
         halo_wait_send(3, AM, PAD, c)
 
     loop(chunks, drain)
+
+
+def copy_out(*refs):
+    sems = refs[6]
+    copies = [
+        pltpu.make_async_copy(refs[i].at[x], refs[3 + i].at[x], sems.at[i, x])
+        for i in range(3)
+        for x in range(refs[i].shape[0])
+    ]
+    for copy in copies:
+        copy.start()
+    for copy in copies:
+        copy.wait()
 
 
 def per_device(n_gx, n_shot, wp, wn, ax, an, velocity, obs, signs, panel, srcpos, wav, recv):
@@ -517,15 +488,13 @@
     dma = pltpu.SemaphoreType.DMA
     n_rec = recv.shape[0]
     cells = cx * ny * nz
-    out_w, out_a, out_g = pl.pallas_call(
+    small = (obs, signs, panel.reshape(1, -1), srcpos, wav.T, recv.reshape(1, -1))
+    shapes = ((cx, ny, nz), (cx, ny, nz), (cx, share, nz))
+    results = pl.pallas_call(
         functools.partial(kernel, n_gx, n_shot),
-        out_shape=(
-            jax.ShapeDtypeStruct((cx, ny, nz), f32),
-            jax.ShapeDtypeStruct((cx, ny, nz), f32),
-            jax.ShapeDtypeStruct((cx, share, nz), f32),
-        ),
-        in_specs=[any_space] * 5 + [vmem] * 6,
-        out_specs=(any_space,) * 3,
+        out_shape=tuple(pltpu.VMEM(shape, f32) for shape in shapes),
+        in_specs=[any_space] * 11,
+        out_specs=(vmem,) * 3,
         scratch_shapes=[
             pltpu.VMEM(field, f32),
             pltpu.VMEM(field, f32),
@@ -534,26 +503,26 @@
             pltpu.VMEM((cx, ny, nz), f32),
             pltpu.VMEM((cx, ny, nz), f32),
             pltpu.VMEM((4, 2, 4, ny, nz), f32),
-            pltpu.VMEM((2, 2, cx, ROWS, nz), f32),
             pltpu.VMEM((n_z, cx, share, nz), f32),
             pltpu.VMEM((n_z, cx, share, nz), f32),
             pltpu.VMEM((5, ny, LANES), f32),
             pltpu.VMEM((n_shot, 8, 2 * n_rec), f32),
             pltpu.VMEM((n_shot, 8, 2 * n_rec), f32),
-            pltpu.VMEM((cx, share, nz), f32),
+            *(pltpu.VMEM(v.shape, v.dtype) for v in small),
             dma((4, 2, chunks)),
             dma((4, 2, chunks)),
+            dma((5,)),
             dma((6,)),
-            dma((2, 2)),
             dma((n_shot,)),
             dma((n_shot,)),
             dma((n_z,)),
             dma((n_z,)),
             dma((n_z,)),
             dma((n_z,)),
+            pltpu.SemaphoreType.REGULAR,
         ],
         compiler_params=pltpu.CompilerParams(
-            collective_id=0, has_side_effects=True, vmem_limit_bytes=60 * 2**20
+            collective_id=0, has_side_effects=True, vmem_limit_bytes=51 * 2**20
         ),
         cost_estimate=pl.CostEstimate(
             flops=4 * 30 * cells, bytes_accessed=4 * 8 * cells, transcendentals=0
@@ -564,13 +533,17 @@
         ax.reshape(cx, ny, nz),
         an.reshape(cx, ny, nz),
         velocity,
-        obs,
-        signs,
-        panel.reshape(1, -1),
-        srcpos,
-        wav,
-        recv.reshape(1, -1),
+        *small,
     )
+    out_w, out_a, out_g = pl.pallas_call(
+        copy_out,
+        out_shape=tuple(jax.ShapeDtypeStruct(shape, f32) for shape in shapes),
+        in_specs=[vmem] * 3,
+        out_specs=(any_space,) * 3,
+        scratch_shapes=[dma((3, cx))],
+        compiler_params=pltpu.CompilerParams(vmem_limit_bytes=2**20),
+        cost_estimate=pl.CostEstimate(flops=0, bytes_accessed=8 * 4 * cells, transcendentals=0),
+    )(*(pltpu.with_memory_space_constraint(v, pltpu.VMEM) for v in results))
     return out_w[None], out_a[None], out_g
 
 

time: 204 us -> 191 us (0.936); the launches traced: 200 us -> 191 us
  local copies, waits for them, and re-layouts: 9.01 us -> 0 us
    unnamed x8 -> x0, local copies, waits for them, and re-layouts: 9.01 us -> none
    pallas_call x1 -> x2, Pallas kernels: 190 us -> 190 us  [the longest x1 187 us: per_device(): pl.pallas_call(functools.partial(kernel, n_gx, n_shot), out_shape=tuple((...]
where the time goes in v2:
time: 191 us
  Pallas kernels  190 us (99%)
    pallas_call x1, Pallas kernels, per_device(): pl.pallas_call(functools.partial(kernel, n_gx, n_shot), out_shape=tuple((...  187 us

profile of v2, /device:TPU:102, one launch (start us, length us, event | category | flops | bytes accessed | tf_op | source)
XLA Modules:
  0.0 191.0 jit_solution(8023120026680342018)
XLA Ops:
  0.6 186.8 %shard_map.130 = (f32[8,512,256]{2,1,0:T(8,128)S(1)}, f32[8,512,256]{2,1,0:T(8,128)S(1)}, f32[8,64,256]{2,1,0:T(8,128)S(1)}) custom-call(f32[8,512,256]{2,1,0:T(8,128)} %bitcast.9, f32[8,512,256]{2,1,0:T(8,128)} %bitcast.10, f32[8,512,256]{2,1,0:T(8,128)} %bitcast.11, f32[8,512,256]{2,1,0:T(8,128)} %bitcast.12, f32[8,512,256]{2,1,0:T(8,128)} %refs_4_.1, ...), custom_call_target="tpu_custom_call" | custom-call | flops 125829120 | bytes 33554432 | tf_op jit(solution)/shard_map/pallas_call | solution.py:493
  187.4 3.6 %shard_map.131 = (f32[8,512,256]{2,1,0:T(8,128)}, f32[8,512,256]{2,1,0:T(8,128)}, f32[8,64,256]{2,1,0:T(8,128)}) custom-call(f32[8,512,256]{2,1,0:T(8,128)S(1)} %get-tuple-element.9.refs_0_, f32[8,512,256]{2,1,0:T(8,128)S(1)} %get-tuple-element.10.refs_1_, f32[8,64,256]{2,1,0:T(8,128)S(1)} %get-tuple-element.11.refs_2_), custom_call_target="tpu_custom_call" | custom-call | bytes 33554432 | tf_op jit(solution)/shard_map/pallas_call | solution.py:538

commit v3 on v2

--- a/solution.py
+++ b/solution.py
@@ -12,7 +12,8 @@
 COEFS = (-205.0 / 72.0, 8.0 / 5.0, -1.0 / 5.0, 8.0 / 315.0, -1.0 / 560.0)
 STEP_RATIO = 0.09
 PAD = 8
-ROWS = 64
+PARTS = (((0, 8),), ((0, 8),), ((0, 4), (4, 4)), ((0, 7), (7, 1)))
+FIRST = (0, 1, 2, 4, 6)
 LANES = 128
 DEEP = 8
 S0, S1, NR, D1, D2 = range(5)
@@ -36,11 +37,9 @@
     WN, AN, WM, AM, VEL, IMG, halo, recv1, recv2, compact, psend, precv = refs[14:26]
     small_vmem = refs[26:32]
     obs, signs, panel, srcpos, wav, recv = small_vmem
-    ssem, rsem, lsem, isem, esem, ersem, s1sem, r1sem, s2sem, r2sem, ready = refs[32:]
+    ssem, rsem, isem, esem, ersem, s1sem, r1sem, s2sem, r2sem, ready = refs[32:]
     cx, ny, nz = VEL.shape
-    chunks = ny // ROWS
     share = ny // n_shot
-    per_block = share // ROWS
     n_z = n_shot // 2
     g = lax.axis_index("gx")
     s = lax.axis_index("shot")
@@ -77,39 +76,52 @@
     neighbours = has[0].astype(jnp.int32) + has[1].astype(jnp.int32)
     pl.semaphore_wait(barrier, neighbours + rank)
 
-    def rows_of(c, offset=0):
-        return pl.ds(pl.multiple_of(c * ROWS + offset, 8), ROWS)
-
-    def halo_copy(h, src, offset, c, d, slot):
+    def halo_copy(h, i, d, slot):
+        unit, count = PARTS[h][i]
+        source, first = ((wn, 0), (an, 0), (WM, PAD), (AM, PAD))[h]
         return pltpu.make_async_remote_copy(
-            src_ref=src.at[pl.ds(4 * d, 4), rows_of(c, offset), :],
-            dst_ref=halo.at[h, slot, :, rows_of(c), :],
-            send_sem=ssem.at[h, d, c],
-            recv_sem=rsem.at[h, slot, c],
+            src_ref=source.at[pl.ds(4 * d, 4), pl.ds(first + unit * share, count * share), :],
+            dst_ref=halo.at[h, slot, :, pl.ds(unit * share, count * share), :],
+            send_sem=ssem.at[d, FIRST[h] + i],
+            recv_sem=rsem.at[slot, FIRST[h] + i],
             device_id=(g + 2 * d - 1, s),
             device_id_type=MESH,
         )
 
-    def halo_start(h, src, offset, c):
+    def halo_start(h, i):
         for d in range(2):
 
             @pl.when(has[d])
             def _():
-                halo_copy(h, src, offset, c, d, 1 - d).start()
-
-    def halo_wait_recv(h, src, offset, c):
+                halo_copy(h, i, d, 1 - d).start()
+
+    def halo_wait_recv(h, i):
         for d in range(2):
 
             @pl.when(has[d])
             def _():
-                halo_copy(h, src, offset, c, d, d).wait_recv()
-
-    def halo_wait_send(h, src, offset, c):
+                halo_copy(h, i, d, d).wait_recv()
+
+    def halo_wait_send(h, i):
         for d in range(2):
 
             @pl.when(has[d])
             def _():
-                halo_copy(h, src, offset, c, d, 1 - d).wait_send()
+                halo_copy(h, i, d, 1 - d).wait_send()
+
+    def start_behind(h, u):
+        for i, (unit, count) in enumerate(PARTS[h]):
+
+            @pl.when(u == unit + count - 1)
+            def _():
+                halo_start(h, i)
+
+    def wait_ahead(h, u):
+        for i, (unit, _) in enumerate(PARTS[h]):
+
+            @pl.when(u == unit)
+            def _():
+                halo_wait_recv(h, i)
 
     def loop(n, body):
         def step(i, carry):
@@ -118,28 +130,28 @@
 
         lax.fori_loop(0, n, step, 0)
 
-    loop(chunks, lambda c: halo_start(0, wn, 0, c))
-
+    halo_start(0, 0)
+    halo_start(1, 0)
+
+    for r in range(n_shot - 1):
+
+        @pl.when(rank > r)
+        def _():
+            pl.semaphore_signal(ready, inc=1, device_id=(g, peer(r)), device_id_type=MESH)
+
+
+    for copy in gathers:
+        copy.wait()
     inner = pl.ds(PAD, ny)
     loads = [
-        pltpu.make_async_copy(wn, WN.at[:, inner, :], lsem.at[0]),
-        pltpu.make_async_copy(vel_hbm, VEL, lsem.at[1]),
-        pltpu.make_async_copy(wp, WM.at[:, inner, :], lsem.at[2]),
-        pltpu.make_async_copy(an, AN.at[:, inner, :], lsem.at[3]),
-        pltpu.make_async_copy(ax, AM.at[:, inner, :], lsem.at[4]),
+        pltpu.make_async_copy(wn, WN.at[:, inner, :], isem.at[0]),
+        pltpu.make_async_copy(vel_hbm, VEL, isem.at[1]),
+        pltpu.make_async_copy(wp, WM.at[:, inner, :], isem.at[2]),
+        pltpu.make_async_copy(an, AN.at[:, inner, :], isem.at[3]),
+        pltpu.make_async_copy(ax, AM.at[:, inner, :], isem.at[4]),
     ]
     for copy in loads:
         copy.start()
-    loop(chunks, lambda c: halo_start(1, an, 0, c))
-    for r in range(n_shot - 1):
-
-        @pl.when(rank > r)
-        def _():
-            pl.semaphore_signal(ready, inc=1, device_id=(g, peer(r)), device_id_type=MESH)
-
-
-    for copy in gathers:
-        copy.wait()
     n_shots = signs.shape[1]
     sign_float = signs[...].astype(jnp.float32)
     shot_row = lax.broadcasted_iota(jnp.int32, (n_shots, n_shots), 0)
@@ -162,9 +174,9 @@
         to = lax.rem(s + k, n_shot)
         return pltpu.make_async_remote_copy(
             src_ref=psend.at[to],
-            dst_ref=precv.at[k],
-            send_sem=esem.at[k],
-            recv_sem=ersem.at[k],
+            dst_ref=precv.at[k - 1],
+            send_sem=esem.at[k - 1],
+            recv_sem=ersem.at[k - 1],
             device_id=(g, to),
             device_id_type=MESH,
         )
@@ -227,7 +239,7 @@
     total = psend[s]
     for k in range(1, n_shot):
         panel_copy(k).wait_recv()
-        total = total + precv[k]
+        total = total + precv[k - 1]
     compact[D1] = spread(rec_hot, total[0:1, :n_rec], rec_code)
     compact[D2] = spread(rec_hot, total[0:1, n_rec:], rec_code)
 
@@ -273,13 +285,13 @@
 
     halves = (pl.ds(0, LANES), pl.ds(LANES, LANES))
 
-    def over_rows(c, body):
+    def over_rows(c, count, body):
         def block(i):
-            row = c * ROWS + i * 8
+            row = c * count + i * 8
             for x in range(cx):
-                body(x, row, i)
-
-        loop(ROWS // 8, block)
+                body(x, row)
+
+        loop(count // 8, block)
 
     def here(row):
         return pl.ds(pl.multiple_of(row, 8), 8)
@@ -290,7 +302,7 @@
     for i in (0, 1, 2):
         loads[i].wait()
 
-    def first(x, row, i):
+    def first(x, row):
         centre, lap = laplacian(WN, 0, x, row)
         lap[0] = lap[0] + jnp.where(deep, compact_at(S0, x, row), 0.0)
         for half in range(2):
@@ -299,17 +311,17 @@
             WM[at] = 2.0 * centre[half] - WM[at] + change
             IMG[x, here(row), halves[half]] = change
 
-    def first_chunk(c):
-        halo_wait_recv(0, wn, 0, c)
-        over_rows(c, first)
-        halo_start(2, WM, PAD, c)
-
-    loop(chunks, first_chunk)
+    def first_unit(u):
+        over_rows(u, share, first)
+        start_behind(2, u)
+
+    halo_wait_recv(0, 0)
+    loop(n_shot, first_unit)
 
     for i in (3, 4):
         loads[i].wait()
 
-    def second(x, row, i):
+    def second(x, row):
         centre, lap = laplacian(AN, 1, x, row)
         inject = compact_at(NR, x, row) * WM[x, padded(row), halves[0]] - compact_at(D2, x, row)
         lap[0] = lap[0] + jnp.where(deep, inject, 0.0)
@@ -320,12 +332,12 @@
             at = (x, here(row), halves[half])
             IMG[at] = IMG[at] * value
 
-    def second_chunk(c):
-        halo_wait_recv(1, an, 0, c)
-        over_rows(c, second)
-        halo_start(3, AM, PAD, c)
-
-    loop(chunks, second_chunk)
+    def second_unit(u):
+        over_rows(u, share, second)
+        start_behind(3, u)
+
+    halo_wait_recv(1, 0)
+    loop(n_shot, second_unit)
 
     def pair_copy(j, block):
         return pltpu.make_async_remote_copy(
@@ -364,7 +376,7 @@
         def _():
             ring_copy(j, z).start()
 
-    def third(x, row, i):
+    def third(x, row):
         centre, lap = laplacian(WM, 2, x, row)
         lap[0] = lap[0] + jnp.where(deep, compact_at(S1, x, row), 0.0)
         for half in range(2):
@@ -374,13 +386,9 @@
             out_w[image] = 2.0 * centre[half] - WN[at] + change
             IMG[image] = IMG[image] + AN[at] * change
 
-    def third_chunk(c):
-        halo_wait_recv(2, WM, PAD, c)
-        over_rows(c, third)
-
     def third_block(b):
-        for i in range(per_block):
-            third_chunk(b * per_block + i)
+        wait_ahead(2, b)
+        over_rows(b, share, third)
 
         @pl.when(lax.rem(b, 2) != core)
         def _():
@@ -393,7 +401,7 @@
     loop(n_shot, third_block)
     image_share(n_z - 1)
 
-    def fourth(x, row, i):
+    def fourth(x, row):
         centre, lap = laplacian(AM, None, x, row)
         inject = compact_at(NR, x, row) * WN[x, padded(row), halves[0]] - compact_at(D1, x, row)
         lap[0] = lap[0] + jnp.where(deep, inject, 0.0)
@@ -404,9 +412,9 @@
                 + courant_at(x, row, half) * lap[half]
             )
 
-    loop(chunks, lambda c: over_rows(c, fourth))
-
-    def fourth_halo(x, row, i):
+    over_rows(0, ny, fourth)
+
+    def fourth_halo(x, row):
         side = int(x >= cx // 2)
         for half in range(2):
             more = 0.0
@@ -415,10 +423,6 @@
                 more = more + COEFS[k] * halo[3, side, p, here(row), halves[half]]
             at = (x, here(row), halves[half])
             out_a[at] = out_a[at] + courant_at(x, row, half) * more
-
-    def fourth_chunk(c):
-        halo_wait_recv(3, AM, PAD, c)
-        over_rows(c, fourth_halo)
 
     def finish_image():
         for k in range(1, n_z):
@@ -436,15 +440,16 @@
 
         loop(share // 8, add)
 
-    def fourth_step(c):
-        @pl.when(c == chunks - 1)
-        def _():
-            finish_image()
-
-        fourth_chunk(c)
-
-    loop(chunks, fourth_step)
-
+    last = len(PARTS[3]) - 1
+    tail = PARTS[3][last][0]
+
+    def fourth_unit(u):
+        wait_ahead(3, u)
+        over_rows(u, share, fourth_halo)
+
+    loop(tail, fourth_unit)
+
+    finish_image()
     for k in range(1, n_shot):
         panel_copy(k).wait_send()
     for j in range(n_z):
@@ -454,21 +459,23 @@
         def _():
             ring_copy(j, z).wait_send()
 
-    def drain(c):
-        halo_wait_send(0, wn, 0, c)
-        halo_wait_send(1, an, 0, c)
-        halo_wait_send(2, WM, PAD, c)
-        halo_wait_send(3, AM, PAD, c)
-
-    loop(chunks, drain)
+    for h in range(4):
+        for i in range(len(PARTS[h])):
+            if (h, i) != (3, last):
+                halo_wait_send(h, i)
+    halo_wait_recv(3, last)
+    loop(n_shot - tail, lambda u: over_rows(u + tail, share, fourth_halo))
+    halo_wait_send(3, last)
 
 
 def copy_out(*refs):
     sems = refs[6]
+    half = refs[0].shape[0] // 2
+    parts = [(i, pl.ds(n * half, half)) for i in range(2) for n in range(2)]
+    parts.append((2, slice(None)))
     copies = [
-        pltpu.make_async_copy(refs[i].at[x], refs[3 + i].at[x], sems.at[i, x])
-        for i in range(3)
-        for x in range(refs[i].shape[0])
+        pltpu.make_async_copy(refs[i].at[part], refs[3 + i].at[part], sems.at[n])
+        for n, (i, part) in enumerate(parts)
     ]
     for copy in copies:
         copy.start()
@@ -478,7 +485,6 @@
 
 def per_device(n_gx, n_shot, wp, wn, ax, an, velocity, obs, signs, panel, srcpos, wav, recv):
     cx, ny, nz = velocity.shape
-    chunks = ny // ROWS
     share = ny // n_shot
     n_z = n_shot // 2
     f32 = jnp.float32
@@ -507,14 +513,13 @@
             pltpu.VMEM((n_z, cx, share, nz), f32),
             pltpu.VMEM((5, ny, LANES), f32),
             pltpu.VMEM((n_shot, 8, 2 * n_rec), f32),
-            pltpu.VMEM((n_shot, 8, 2 * n_rec), f32),
+            pltpu.VMEM((n_shot - 1, 8, 2 * n_rec), f32),
             *(pltpu.VMEM(v.shape, v.dtype) for v in small),
-            dma((4, 2, chunks)),
-            dma((4, 2, chunks)),
-            dma((5,)),
+            dma((2, FIRST[4])),
+            dma((2, FIRST[4])),
             dma((6,)),
-            dma((n_shot,)),
-            dma((n_shot,)),
+            dma((n_shot - 1,)),
+            dma((n_shot - 1,)),
             dma((n_z,)),
             dma((n_z,)),
             dma((n_z,)),
@@ -540,7 +545,7 @@
         out_shape=tuple(jax.ShapeDtypeStruct(shape, f32) for shape in shapes),
         in_specs=[vmem] * 3,
         out_specs=(any_space,) * 3,
-        scratch_shapes=[dma((3, cx))],
+        scratch_shapes=[dma((5,))],
         compiler_params=pltpu.CompilerParams(vmem_limit_bytes=2**20),
         cost_estimate=pl.CostEstimate(flops=0, bytes_accessed=8 * 4 * cells, transcendentals=0),
     )(*(pltpu.with_memory_space_constraint(v, pltpu.VMEM) for v in results))

time: 191 us -> 190 us (level)
  no operation moved by 1% of the time
where the time goes in v3:
time: 190 us
  Pallas kernels  189 us (99%)
    pallas_call x1, Pallas kernels, per_device(): pl.pallas_call(functools.partial(kernel, n_gx, n_shot), out_shape=tuple((...  186 us

profile of v3, /device:TPU:102, one launch (start us, length us, event | category | flops | bytes accessed | tf_op | source)
XLA Modules:
  0.0 189.8 jit_solution(14025586898567489307)
XLA Ops:
  0.6 185.7 %shard_map.130 = (f32[8,512,256]{2,1,0:T(8,128)S(1)}, f32[8,512,256]{2,1,0:T(8,128)S(1)}, f32[8,64,256]{2,1,0:T(8,128)S(1)}) custom-call(f32[8,512,256]{2,1,0:T(8,128)} %bitcast.9, f32[8,512,256]{2,1,0:T(8,128)} %bitcast.10, f32[8,512,256]{2,1,0:T(8,128)} %bitcast.11, f32[8,512,256]{2,1,0:T(8,128)} %bitcast.12, f32[8,512,256]{2,1,0:T(8,128)} %refs_4_.1, ...), custom_call_target="tpu_custom_call" | custom-call | flops 125829120 | bytes 33554432 | tf_op jit(solution)/shard_map/pallas_call | solution.py:499
  186.3 3.5 %shard_map.131 = (f32[8,512,256]{2,1,0:T(8,128)}, f32[8,512,256]{2,1,0:T(8,128)}, f32[8,64,256]{2,1,0:T(8,128)}) custom-call(f32[8,512,256]{2,1,0:T(8,128)S(1)} %get-tuple-element.9.refs_0_, f32[8,512,256]{2,1,0:T(8,128)S(1)} %get-tuple-element.10.refs_1_, f32[8,64,256]{2,1,0:T(8,128)S(1)} %get-tuple-element.11.refs_2_), custom_call_target="tpu_custom_call" | custom-call | bytes 33554432 | tf_op jit(solution)/shard_map/pallas_call | solution.py:543

commit v4 on v3

--- a/solution.py
+++ b/solution.py
@@ -34,10 +34,10 @@
 def kernel(n_gx, n_shot, *refs):
     (wp, wn, ax, an, vel_hbm), small = refs[:5], refs[5:11]
     out_w, out_a, ograd = refs[11:14]
-    WN, AN, WM, AM, VEL, IMG, halo, recv1, recv2, compact, psend, precv = refs[14:26]
-    small_vmem = refs[26:32]
+    WN, AN, WM, AM, VEL, IMG, halo, recv1, recv2, compact, psend, ppair, psum, precv = refs[14:28]
+    small_vmem = refs[28:34]
     obs, signs, panel, srcpos, wav, recv = small_vmem
-    ssem, rsem, isem, esem, ersem, s1sem, r1sem, s2sem, r2sem, ready = refs[32:]
+    ssem, rsem, isem, esem, ersem, s1sem, r1sem, s2sem, r2sem, ready = refs[34:]
     cx, ny, nz = VEL.shape
     share = ny // n_shot
     n_z = n_shot // 2
@@ -48,7 +48,6 @@
     sibling = s + 1 - 2 * core
     has = (g > 0, g < n_gx - 1)
 
-    rank = 2 * z + 1 - core
     barrier = pltpu.get_barrier_semaphore()
     for d in range(2):
 
@@ -58,14 +57,15 @@
                 barrier, inc=1, device_id=(g + 2 * d - 1, s), device_id_type=MESH
             )
 
-    def peer(r):
-        return 2 * lax.div(r, 2) + 1 - lax.rem(r, 2)
-
-    for r in range(1, n_shot):
-
-        @pl.when(rank < r)
-        def _():
-            pl.semaphore_signal(barrier, inc=1, device_id=(g, peer(r)), device_id_type=MESH)
+    @pl.when(core == 1)
+    def _():
+        pl.semaphore_signal(barrier, inc=1, device_id=(g, sibling), device_id_type=MESH)
+
+    for q in range(1, n_z):
+
+        @pl.when(z < q)
+        def _():
+            pl.semaphore_signal(barrier, inc=1, device_id=(g, 2 * q + core), device_id_type=MESH)
 
     gathers = [
         pltpu.make_async_copy(source, target, isem.at[i])
@@ -74,7 +74,7 @@
     for copy in gathers:
         copy.start()
     neighbours = has[0].astype(jnp.int32) + has[1].astype(jnp.int32)
-    pl.semaphore_wait(barrier, neighbours + rank)
+    pl.semaphore_wait(barrier, neighbours + z + 1 - core)
 
     def halo_copy(h, i, d, slot):
         unit, count = PARTS[h][i]
@@ -133,12 +133,15 @@
     halo_start(0, 0)
     halo_start(1, 0)
 
-    for r in range(n_shot - 1):
-
-        @pl.when(rank > r)
-        def _():
-            pl.semaphore_signal(ready, inc=1, device_id=(g, peer(r)), device_id_type=MESH)
-
+    @pl.when(core == 0)
+    def _():
+        pl.semaphore_signal(ready, inc=1, device_id=(g, sibling), device_id_type=MESH)
+
+    for q in range(n_z - 1):
+
+        @pl.when(z > q)
+        def _():
+            pl.semaphore_signal(ready, inc=1, device_id=(g, 2 * q + core), device_id_type=MESH)
 
     for copy in gathers:
         copy.wait()
@@ -166,28 +169,38 @@
             mine, obs[:, t, :], precision=HIGHEST, preferred_element_type=jnp.float32
         )
         for q in range(n_shot):
-            psend[q, :, t * n_rec : (t + 1) * n_rec] = jnp.broadcast_to(
+            psend[q % 2, q // 2, :, t * n_rec : (t + 1) * n_rec] = jnp.broadcast_to(
                 part[q : q + 1, :], (8, n_rec)
             )
 
+    def panel_pair():
+        return pltpu.make_async_remote_copy(
+            src_ref=psend.at[1 - core],
+            dst_ref=ppair,
+            send_sem=esem.at[0],
+            recv_sem=ersem.at[0],
+            device_id=(g, sibling),
+            device_id_type=MESH,
+        )
+
     def panel_copy(k):
-        to = lax.rem(s + k, n_shot)
+        to = lax.rem(z + k, n_z)
         return pltpu.make_async_remote_copy(
-            src_ref=psend.at[to],
+            src_ref=psum.at[to],
             dst_ref=precv.at[k - 1],
-            send_sem=esem.at[k - 1],
-            recv_sem=ersem.at[k - 1],
-            device_id=(g, to),
+            send_sem=esem.at[k],
+            recv_sem=ersem.at[k],
+            device_id=(g, 2 * to + core),
             device_id_type=MESH,
         )
 
-
-    @pl.when(rank < n_shot - 1)
+    answers = n_z - 1 - z + core
+
+    @pl.when(answers > 0)
     def _():
-        pl.semaphore_wait(ready, n_shot - 1 - rank)
-
-    for k in range(1, n_shot):
-        panel_copy(k).start()
+        pl.semaphore_wait(ready, answers)
+
+    panel_pair().start()
 
     for field in (WN, AN, WM, AM):
         field[:, 0:PAD, :] = jnp.zeros((cx, PAD, nz), jnp.float32)
@@ -203,6 +216,11 @@
                     )
 
             loop(ny // 8, clear)
+
+    panel_pair().wait_recv()
+    psum[...] = psend[core] + ppair[...]
+    for k in range(1, n_z):
+        panel_copy(k).start()
 
     def one_hot_rows(y):
         return jnp.where(
@@ -236,8 +254,8 @@
     rec_hot = one_hot_rows(rec_y)
     compact[NR] = spread(rec_hot, jnp.ones((1, n_rec), jnp.float32), rec_code)
 
-    total = psend[s]
-    for k in range(1, n_shot):
+    total = psum[z]
+    for k in range(1, n_z):
         panel_copy(k).wait_recv()
         total = total + precv[k - 1]
     compact[D1] = spread(rec_hot, total[0:1, :n_rec], rec_code)
@@ -450,7 +468,8 @@
     loop(tail, fourth_unit)
 
     finish_image()
-    for k in range(1, n_shot):
+    panel_pair().wait_send()
+    for k in range(1, n_z):
         panel_copy(k).wait_send()
     for j in range(n_z):
         pair_copy(j, 2 * j + 1 - core).wait_send()
@@ -512,14 +531,16 @@
             pltpu.VMEM((n_z, cx, share, nz), f32),
             pltpu.VMEM((n_z, cx, share, nz), f32),
             pltpu.VMEM((5, ny, LANES), f32),
-            pltpu.VMEM((n_shot, 8, 2 * n_rec), f32),
-            pltpu.VMEM((n_shot - 1, 8, 2 * n_rec), f32),
+            pltpu.VMEM((2, n_z, 8, 2 * n_rec), f32),
+            pltpu.VMEM((n_z, 8, 2 * n_rec), f32),
+            pltpu.VMEM((n_z, 8, 2 * n_rec), f32),
+            pltpu.VMEM((n_z - 1, 8, 2 * n_rec), f32),
             *(pltpu.VMEM(v.shape, v.dtype) for v in small),
             dma((2, FIRST[4])),
             dma((2, FIRST[4])),
             dma((6,)),
-            dma((n_shot - 1,)),
-            dma((n_shot - 1,)),
+            dma((n_z,)),
+            dma((n_z,)),
             dma((n_z,)),
             dma((n_z,)),
             dma((n_z,)),

time: 190 us -> 190 us (level)
  no operation moved by 1% of the time
where the time goes in v4:
time: 190 us; the launch traced here: 189 us
  Pallas kernels  189 us (99%)
    pallas_call x1, Pallas kernels, per_device(): pl.pallas_call(functools.partial(kernel, n_gx, n_shot), out_shape=tuple((...  185 us

profile of v4, /device:TPU:102, one launch (start us, length us, event | category | flops | bytes accessed | tf_op | source)
XLA Modules:
  0.0 189.4 jit_solution(4858423256100473316)
XLA Ops:
  0.6 185.3 %shard_map.130 = (f32[8,512,256]{2,1,0:T(8,128)S(1)}, f32[8,512,256]{2,1,0:T(8,128)S(1)}, f32[8,64,256]{2,1,0:T(8,128)S(1)}) custom-call(f32[8,512,256]{2,1,0:T(8,128)} %bitcast.9, f32[8,512,256]{2,1,0:T(8,128)} %bitcast.10, f32[8,512,256]{2,1,0:T(8,128)} %bitcast.11, f32[8,512,256]{2,1,0:T(8,128)} %bitcast.12, f32[8,512,256]{2,1,0:T(8,128)} %refs_4_.1, ...), custom_call_target="tpu_custom_call" | custom-call | flops 125829120 | bytes 33554432 | tf_op jit(solution)/shard_map/pallas_call | solution.py:518
  185.9 3.5 %shard_map.131 = (f32[8,512,256]{2,1,0:T(8,128)}, f32[8,512,256]{2,1,0:T(8,128)}, f32[8,64,256]{2,1,0:T(8,128)}) custom-call(f32[8,512,256]{2,1,0:T(8,128)S(1)} %get-tuple-element.9.refs_0_, f32[8,512,256]{2,1,0:T(8,128)S(1)} %get-tuple-element.10.refs_1_, f32[8,64,256]{2,1,0:T(8,128)S(1)} %get-tuple-element.11.refs_2_), custom_call_target="tpu_custom_call" | custom-call | bytes 33554432 | tf_op jit(solution)/shard_map/pallas_call | solution.py:564
